TPU v7x, 128 devices: a whole 4x4x4 slice. The times are simulated.
128 devices in a mesh: dp: 8 (over z_lo, x), fsdp: 16 (over y, z_hi, core).
Axes of the slice: x: 4, y: 4, z: 4 (z_hi: 2, z_lo: 2; z = z_hi * 2 + z_lo), core: 2. Of those that a mesh axis runs over, the one named last changes fastest.
Arguments:
- queries: bfloat16 [65536, 2048], P(('dp', 'fsdp')), may hold values from -6 to 6
- keys: bfloat16 [65536, 2048], P(('dp', 'fsdp')), may hold values from -6 to 6
- values: bfloat16 [65536, 2048], P(('dp', 'fsdp')), may hold values from -6 to 6
- attn_out: bfloat16 [65536, 2048], P(('dp', 'fsdp')), may hold values from -24 to 24
- out_grad: bfloat16 [65536, 2048], P(('dp', 'fsdp')), may hold values from -6 to 6
- log_norm: float32 [65536, 16], P(('dp', 'fsdp')), may hold values from 4 to 7
- segment_ids: int32 [128, 4], P(('dp', 'fsdp')), may hold values from 0 to 3, as said below
- kept_tokens: int32 [128, 4], P(('dp', 'fsdp')), may hold values from 0 to 512, as said below
- out_weight: bfloat16 [2048, 2048], P('fsdp'), may hold values from -0.125 to 0.125
Outputs:
- query_grad: bfloat16 [65536, 2048], P(('dp', 'fsdp'))
- key_grad: bfloat16 [65536, 2048], P(('dp', 'fsdp'))
- value_grad: bfloat16 [65536, 2048], P(('dp', 'fsdp'))
- weight_grad: float32 [2048, 2048], P('fsdp')
Inputs may be any that keep to these rules, and one draw needn't show every extreme that they name: `segment_ids`: row p numbers the images of pack p block by block: 0 for block 0, rising by one at each block that starts a new image. Some pack is one image, some pack has one image a block. `kept_tokens`: entry (p, i) counts the kept tokens of image i of pack p, which fill the start of that image's blocks: an image of b blocks keeps 128 (b - 1) + 1 to 128 b tokens; numbers with no image hold 0.
All inputs are finite; a program needn't handle non-finite values.
Results may differ from a plain program's by a relative error of at most 0.012.
The roundings to bfloat16 on the way count: a program that leaves them out, or rounds other values in their place, can miss the bound.
Values may be sent and summed in bfloat16 or wider, within the bound.
A program may use at most 192 MiB of HBM per device.

v0:
```python
import jax
import jax.numpy as jnp
from jax import lax
from jax.sharding import PartitionSpec as P

BLOCK = 128


def pair_grads(query_heads, key_heads, value_heads, grad_heads, norm_rows, delta_rows, key_live):
    score_scale = query_heads.shape[2] ** (-0.5)
    scores = (
        jnp.einsum("hqd,hkd->hqk", query_heads, key_heads, preferred_element_type=jnp.float32)
        * score_scale
    )
    probs = jnp.where(key_live[None, None, :], jnp.exp(scores - norm_rows[:, :, None]), 0.0)
    value_grad = jnp.einsum(
        "hqk,hqd->hkd", probs.astype(jnp.bfloat16), grad_heads, preferred_element_type=jnp.float32
    )
    prob_grad = jnp.einsum(
        "hqd,hkd->hqk", grad_heads, value_heads, preferred_element_type=jnp.float32
    )
    score_grad = (probs * (prob_grad - delta_rows[:, :, None])).astype(jnp.bfloat16)
    query_grad = (
        jnp.einsum("hqk,hkd->hqd", score_grad, key_heads, preferred_element_type=jnp.float32)
        * score_scale
    )
    key_grad = (
        jnp.einsum("hqk,hqd->hkd", score_grad, query_heads, preferred_element_type=jnp.float32)
        * score_scale
    )
    return (query_grad, key_grad, value_grad)


def to_blocks(rows, block_count, head_count):
    return rows.reshape(block_count, BLOCK, head_count, rows.shape[1] // head_count).transpose(
        0, 2, 1, 3
    )


def from_blocks(blocked):
    block_count, head_count, block_rows, head_size = blocked.shape
    return (
        blocked.transpose(0, 2, 1, 3)
        .reshape(block_count * block_rows, head_count * head_size)
        .astype(jnp.bfloat16)
    )


def per_device(
    queries, keys, values, attn_out, out_grad, log_norm, segment_ids, kept_tokens, out_weight
):
    tok_rows = queries.shape[0]
    feat_width = queries.shape[1]
    head_count = log_norm.shape[1]
    head_size = feat_width // head_count
    block_count = tok_rows // BLOCK
    seg_ids = segment_ids[0]
    kept_counts = kept_tokens[0]
    block_ids = jnp.arange(block_count)
    first_block = jnp.sum((seg_ids[None, :] < seg_ids[:, None]).astype(jnp.int32), axis=1)
    block_kept = jnp.sum(
        (seg_ids[:, None] == block_ids[None, :]).astype(jnp.int32) * kept_counts[None, :], axis=1
    )
    positions = (block_ids - first_block)[:, None] * BLOCK + jnp.arange(BLOCK)[None, :]
    block_valid = positions < block_kept[:, None]
    token_valid = block_valid.reshape(tok_rows)
    grad_input = jnp.where(token_valid[:, None], out_grad, jnp.zeros_like(out_grad))
    attn_grad = lax.dot_general(
        grad_input,
        lax.all_gather(out_weight, "fsdp", axis=0, tiled=True),
        (((1,), (1,)), ((), ())),
        preferred_element_type=jnp.float32,
    ).astype(jnp.bfloat16)
    delta = jnp.sum(
        (attn_grad.astype(jnp.float32) * attn_out.astype(jnp.float32)).reshape(
            tok_rows, head_count, head_size
        ),
        axis=2,
    )
    grad_share = lax.psum_scatter(
        lax.dot_general(
            attn_out, grad_input, (((0,), (0,)), ((), ())), preferred_element_type=jnp.float32
        ),
        "fsdp",
        scatter_dimension=0,
        tiled=True,
    )
    weight_grad = lax.psum(grad_share, "dp")
    query_blocks = to_blocks(queries, block_count, head_count)
    key_blocks = to_blocks(keys, block_count, head_count)
    value_blocks = to_blocks(values, block_count, head_count)
    grad_blocks = to_blocks(attn_grad, block_count, head_count)
    norm_blocks = log_norm.reshape(block_count, BLOCK, head_count).transpose(0, 2, 1)
    delta_blocks = delta.reshape(block_count, BLOCK, head_count).transpose(0, 2, 1)
    pair_ids = jnp.arange(block_count * block_count)
    pair_live = (seg_ids[pair_ids // block_count] == seg_ids[pair_ids % block_count]).astype(
        jnp.int32
    )
    pair_order = jnp.argsort(1 - pair_live, stable=True)
    pair_total = jnp.sum(pair_live)

    def take_blocks(query_block, key_block):
        return (
            query_blocks[query_block],
            key_blocks[key_block],
            value_blocks[key_block],
            grad_blocks[query_block],
            norm_blocks[query_block],
            delta_blocks[query_block],
            block_valid[key_block],
        )

    def run_pair(pair_step, totals):
        pair_index = pair_order[pair_step]
        query_block = pair_index // block_count
        key_block = pair_index % block_count
        query_term, key_term, value_term = pair_grads(*take_blocks(query_block, key_block))
        return (
            totals[0].at[query_block].add(query_term),
            totals[1].at[key_block].add(key_term),
            totals[2].at[key_block].add(value_term),
        )

    empty = jnp.zeros((block_count, head_count, BLOCK, head_size), jnp.float32)
    totals = (empty, empty, empty)
    totals = lax.fori_loop(0, pair_total, run_pair, totals)
    return (from_blocks(totals[0]), from_blocks(totals[1]), from_blocks(totals[2]), weight_grad)


def solution(mesh):
    placed = (
        P(("dp", "fsdp"), None),
        P(("dp", "fsdp"), None),
        P(("dp", "fsdp"), None),
        P(("dp", "fsdp"), None),
        P(("dp", "fsdp"), None),
        P(("dp", "fsdp"), None),
        P(("dp", "fsdp"), None),
        P(("dp", "fsdp"), None),
        P("fsdp", None),
    )
    return jax.shard_map(
        per_device,
        mesh=mesh,
        in_specs=placed,
        out_specs=(
            P(("dp", "fsdp"), None),
            P(("dp", "fsdp"), None),
            P(("dp", "fsdp"), None),
            P("fsdp", None),
        ),
        check_vma=False,
    )
```

profile of v0, /device:TPU:0, one launch (start us, length us, event | category | flops | bytes accessed | tf_op | source)
XLA Modules:
  0.0 482.5 jit_solution(11948150179926760325)
XLA Ops:
  9.0 12.6 %convolution_bitcast_fusion.1 = f32[2048,2048]{0,1:T(8,128)} fusion(bf16[512,2048]{1,0:T(8,128)(2,1)} %param.20, bf16[512,2048]{1,0:T(8,128)(2,1)} %param.21, pred[512]{0:T(512)(128)(4,1)S(1)} %fusion.27), kind=kOutput, calls=%fused_computation.45 | convolution fusion | flops 4296015872 | bytes 20972032 | tf_op jit(solution)/shard_map/dot_general | solution.py:81
  37.7 48.0 %all-gather.2.cloned.1.call-done = bf16[2048,2048]{1,0:T(8,128)(2,1)} async-done(((bf16[128,2048]{1,0:T(8,128)(2,1)}), bf16[2048,2048]{1,0:T(8,128)(2,1)}) %all-gather.2.cloned.1.call-update) | async-done | bytes 8388624 | tf_op jit(solution)/shard_map/all_gather | solution.py:70
  85.7 8.4 %convolution_convert_fusion = bf16[512,2048]{1,0:T(8,128)(2,1)S(1)} fusion(bf16[2048,2048]{1,0:T(8,128)(2,1)} %all-gather.2.cloned.1.call-done, bf16[512,2048]{1,0:T(8,128)(2,1)S(1)} %copy-done.10, pred[512]{0:T(512)(128)(4,1)S(1)} %fusion.27), kind=kOutput, calls=%fused_computation.47 | convolution fusion | flops 4297064448 | bytes 12583424 | tf_op jit(solution)/shard_map/dot_general | solution.py:68
  100.6 4.1 reduce_sum.39
  113.1 286.7 %while.19 = (s32[]{:T(128)}, f32[4,16,128,128]{3,2,1,0:T(8,128)}, f32[4,16,128,128]{3,2,1,0:T(8,128)}, f32[4,16,128,128]{3,2,1,0:T(8,128)}, s32[]{:T(128)}, /*in...) while((s32[]{:T(128)}, f32[4,16,128,128]{3,2,1,0:T(8,128)}, ...), condition=%wide.region_8.9_spmd, body=%wide.region_5.8_spmd.sunk | while | flops 339476544 | bytes 17879468 | solution.py:126
  121.6 3.3 fusion.49
  124.9 3.2 fusion.47
  128.1 3.5 fusion.48
  139.8 3.2 fusion.49
  143.0 3.2 fusion.47
  146.2 3.3 fusion.48
  157.7 3.2 fusion.49
  161.0 3.2 fusion.47
  164.2 3.2 fusion.48
  175.6 3.2 fusion.49
  178.8 3.2 fusion.47
  182.0 3.2 fusion.48
  193.4 3.3 fusion.49
  196.7 3.3 fusion.47
  200.0 3.2 fusion.48
  211.5 3.2 fusion.49
  214.7 3.3 fusion.47
  217.9 3.3 fusion.48
  229.4 3.2 fusion.49
  232.6 3.2 fusion.47
  235.8 3.2 fusion.48
  247.2 3.2 fusion.49
  250.4 3.2 fusion.47
  253.7 3.2 fusion.48
  265.0 3.3 fusion.49
  268.3 3.2 fusion.47
  271.5 3.2 fusion.48
  282.9 3.2 fusion.49
  286.1 3.2 fusion.47
  289.3 3.2 fusion.48
  300.7 3.2 fusion.49
  303.9 3.2 fusion.47
  307.1 3.2 fusion.48
  318.5 3.2 fusion.49
  324.9 3.2 fusion.48
  336.2 3.3 fusion.49
  342.7 3.2 fusion.48
  354.1 3.2 fusion.49
  360.5 3.2 fusion.48
  371.9 3.2 fusion.49
  378.3 3.2 fusion.48
  396.0 3.2 fusion.48
  415.2 58.2 %all-reduce.2.cloned.1.call-done = f32[128,2048]{0,1:T(8,128)} async-done(((f32[128,2048]{0,1:T(8,128)}), f32[128,2048]{0,1:T(8,128)}) %all-reduce.2.cloned.1.call-update) | async-done | bytes 1048592 | tf_op jit(solution)/shard_map/psum | solution.py:88
  (200 shorter events, 148.6 us)
Async XLA Ops:
  7.2 78.5 %all-gather.2.cloned.1.call-start = ((), (), s32[]{:S(2)}) async-start(), calls=%async_computation.1 | async-start | bytes 8912896 | tf_op jit(solution)/shard_map/all_gather | solution.py:70
  7.9 392.0 %reduce-scatter.2.cloned.1.call-start = ((), (), s32[]{:S(2)}) async-start(), calls=%async_computation.2 | async-start | bytes 17825792 | tf_op jit(solution)/shard_map/reduce_scatter | solution.py:80
  21.6 0.7 copy-start
  21.6 2.0 copy-start.8
  21.6 451.8 %all-reduce.2.cloned.1.call-start = ((), (), s32[]{:S(2)}) async-start(), calls=%async_computation.3 | async-start | bytes 2097152 | tf_op jit(solution)/shard_map/psum | solution.py:88
  23.6 2.4 copy-start.5
  26.0 2.0 copy-start.6
  31.9 2.2 copy-start.3
  31.9 3.0 copy-start.4
  35.0 50.8 %copy-start.10 = (bf16[512,2048]{1,0:T(8,128)(2,1)S(1)}, bf16[512,2048]{1,0:T(8,128)(2,1)}, u32[]{:S(2)}) copy-start(bf16[512,2048]{1,0:T(8,128)(2,1)} %param.21) | copy-start | bytes 6291460
  94.7 2.0 copy-start.7
  110.4 2.8 copy-start.9
  403.9 3.0 copy-start.2
  408.6 3.0 copy-start.1
Sparse Core Ops, SparseCore 0:
  10.4 75.2 all-gather.1
  90.1 145.1 reduce-scatter.1
  400.1 73.3 all-reduce.1
where the time goes:
time: 487 us; the launch traced here: 482 us
  matrix products  192 us (39%)
  waiting for transfers between devices  107 us (22%)
  local copies, waits for them, and re-layouts  92.4 us (19%)
  loops' own time  53.1 us (11%)
  other arithmetic  23.7 us (5%)
  between operations  14 us (3%)
    psum x1, waiting for transfers between devices, per_device(): weight_grad = lax.psum(grad_share, 'dp')  58.2 us
    another operation x1, loops' own time, per_device(): totals = lax.fori_loop(0, pair_total, run_pair, totals)  53.1 us
    dot_general x16, matrix products, pair_grads(): jnp.einsum('hqk,hqd->hkd', score_grad, query_heads, preferred_element_typ...  51.7 us
    dot_general x16, matrix products, pair_grads(): jnp.einsum('hqk,hqd->hkd', probs.astype(jnp.bfloat16), grad_heads, prefer...  51.5 us
    dot_general x16, matrix products, pair_grads(): jnp.einsum('hqk,hkd->hqd', score_grad, key_heads, preferred_element_type=...  51.3 us
    all_gather x1, waiting for transfers between devices, per_device(): lax.all_gather(out_weight, 'fsdp', axis=0, tiled=True)  48 us
    unnamed x31, local copies, waits for them, and re-layouts  23.6 us
    dynamic_slice x16, local copies, waits for them, and re-layouts, take_blocks(): value_blocks[key_block]  22.3 us
  transfers between devices with their start and end apart: 3, of which 2 were waited for; matrix products, arithmetic and copies ran while one was open for 62% of the time, Pallas kernels for 0%

commit v1 on v0

--- a/solution.py
+++ b/solution.py
@@ -85,7 +85,7 @@
         scatter_dimension=0,
         tiled=True,
     )
-    weight_grad = lax.psum(grad_share, "dp")
+    weight_grad = jnp.sum(lax.all_gather(grad_share, "dp"), axis=0)
     query_blocks = to_blocks(queries, block_count, head_count)
     key_blocks = to_blocks(keys, block_count, head_count)
     value_blocks = to_blocks(values, block_count, head_count)

time: 487 us -> 599 us (1.23)
  waiting for transfers between devices: 107 us -> 207 us
  other arithmetic: 23.7 us -> 34.7 us
    reduce_scatter x1, waiting for transfers between devices: 0.02 us -> 149 us  [per_device(): lax.psum_scatter(lax.dot_general(attn_out, grad_input, (((0,), (0,)), (()...]
    psum x1 -> x0, waiting for transfers between devices: 58.2 us -> none  [per_device(): weight_grad = lax.psum(grad_share, 'dp')]
    reduce_sum x0 -> x1, other arithmetic: none -> 11.6 us  [per_device(): weight_grad = jnp.sum(lax.all_gather(grad_share, 'dp'), axis=0)]
    all_gather x1, waiting for transfers between devices: 48 us -> 57.5 us  [per_device(): lax.all_gather(out_weight, 'fsdp', axis=0, tiled=True)]
    unnamed x31 -> x32, local copies, waits for them, and re-layouts: 23.6 us -> 26.8 us
  transfers between devices with their start and end apart: 3 -> 3, of which waited for: 2 -> 2; matrix products, arithmetic and copies ran while one was open for 62% -> 48% of each run, Pallas kernels for 0% -> 0%
where the time goes in v1:
time: 599 us; the launch traced here: 594 us
  waiting for transfers between devices  207 us (35%)
  matrix products  191 us (32%)
  local copies, waits for them, and re-layouts  94.2 us (16%)
  loops' own time  52.7 us (9%)
  other arithmetic  34.7 us (6%)
  between operations  14 us (2%)
    reduce_scatter x1, waiting for transfers between devices, per_device(): lax.psum_scatter(lax.dot_general(attn_out, grad_input, (((0,), (0,)), (()...  149 us
    all_gather x1, waiting for transfers between devices, per_device(): lax.all_gather(out_weight, 'fsdp', axis=0, tiled=True)  57.5 us
    another operation x1, loops' own time, per_device(): totals = lax.fori_loop(0, pair_total, run_pair, totals)  52.7 us
    dot_general x16, matrix products, pair_grads(): jnp.einsum('hqk,hkd->hqd', score_grad, key_heads, preferred_element_type=...  51.3 us
    dot_general x16, matrix products, pair_grads(): jnp.einsum('hqk,hqd->hkd', probs.astype(jnp.bfloat16), grad_heads, prefer...  51.2 us
    dot_general x16, matrix products, pair_grads(): jnp.einsum('hqk,hqd->hkd', score_grad, query_heads, preferred_element_typ...  51.2 us
    unnamed x32, local copies, waits for them, and re-layouts  26.8 us
    dynamic_slice x16, local copies, waits for them, and re-layouts, take_blocks(): value_blocks[key_block]  22.2 us
  transfers between devices with their start and end apart: 3, of which 2 were waited for; matrix products, arithmetic and copies ran while one was open for 48% of the time, Pallas kernels for 0%

profile of v1, /device:TPU:0, one launch (start us, length us, event | category | flops | bytes accessed | tf_op | source)
XLA Modules:
  0.0 594.0 jit_solution(10618699884986375182)
XLA Ops:
  8.2 12.6 %convolution_bitcast_fusion.1 = f32[2048,2048]{0,1:T(8,128)} fusion(bf16[512,2048]{1,0:T(8,128)(2,1)} %param.20, bf16[512,2048]{1,0:T(8,128)(2,1)} %param.21, pred[512]{0:T(512)(128)(4,1)S(1)} %fusion.27), kind=kOutput, calls=%fused_computation.45 | convolution fusion | flops 4296015872 | bytes 20972032 | tf_op jit(solution)/shard_map/dot_general | solution.py:81
  21.9 148.8 %reduce-scatter.2.cloned.1.call-done = f32[128,2048]{0,1:T(8,128)} async-done(((f32[2048,2048]{0,1:T(8,128)}), f32[128,2048]{0,1:T(8,128)}) %reduce-scatter.2.cloned.1.call-update) | async-done | bytes 1048592 | tf_op jit(solution)/shard_map/reduce_scatter | solution.py:80
  186.3 57.5 %all-gather.4.cloned.1.call-done = bf16[2048,2048]{1,0:T(8,128)(2,1)} async-done(((bf16[128,2048]{1,0:T(8,128)(2,1)}), bf16[2048,2048]{1,0:T(8,128)(2,1)}) %all-gather.4.cloned.1.call-update) | async-done | bytes 8388624 | tf_op jit(solution)/shard_map/all_gather | solution.py:70
  243.8 8.3 %convolution_convert_fusion = bf16[512,2048]{1,0:T(8,128)(2,1)S(1)} fusion(bf16[2048,2048]{1,0:T(8,128)(2,1)} %all-gather.4.cloned.1.call-done, bf16[512,2048]{1,0:T(8,128)(2,1)S(1)} %copy-done.10, pred[512]{0:T(512)(128)(4,1)S(1)} %fusion.27), kind=kOutput, calls=%fused_computation.48 | convolution fusion | flops 4297064448 | bytes 12583424 | tf_op jit(solution)/shard_map/dot_general | solution.py:68
  258.1 3.4 reduce_sum.48
  268.9 285.0 %while.19 = (s32[]{:T(128)}, f32[4,16,128,128]{3,2,1,0:T(8,128)}, f32[4,16,128,128]{3,2,1,0:T(8,128)}, f32[4,16,128,128]{3,2,1,0:T(8,128)}, s32[]{:T(128)}, /*in...) while((s32[]{:T(128)}, f32[4,16,128,128]{3,2,1,0:T(8,128)}, ...), condition=%wide.region_8.9_spmd, body=%wide.region_5.8_spmd.sunk | while | flops 339476544 | bytes 17879468 | solution.py:126
  277.3 3.2 fusion.49
  280.5 3.3 fusion.47
  283.8 3.3 fusion.48
  295.2 3.3 fusion.49
  298.5 3.3 fusion.47
  313.1 3.2 fusion.49
  316.3 3.3 fusion.47
  319.5 3.2 fusion.48
  330.9 3.2 fusion.49
  334.1 3.3 fusion.47
  337.4 3.2 fusion.48
  348.7 3.2 fusion.49
  351.9 3.2 fusion.47
  355.1 3.2 fusion.48
  366.5 3.2 fusion.49
  369.7 3.2 fusion.47
  384.2 3.2 fusion.49
  387.4 3.2 fusion.47
  401.9 3.2 fusion.49
  405.1 3.2 fusion.47
  408.3 3.2 fusion.48
  419.6 3.2 fusion.49
  422.8 3.2 fusion.47
  426.0 3.2 fusion.48
  437.4 3.2 fusion.49
  440.6 3.2 fusion.47
  455.1 3.2 fusion.49
  458.3 3.2 fusion.47
  472.8 3.2 fusion.49
  476.0 3.2 fusion.47
  479.2 3.2 fusion.48
  490.5 3.2 fusion.49
  493.7 3.2 fusion.47
  496.9 3.2 fusion.48
  508.3 3.2 fusion.49
  511.5 3.2 fusion.47
  526.0 3.2 fusion.49
  529.2 3.2 fusion.47
  543.7 3.2 fusion.49
  550.0 3.2 fusion.48
  569.1 5.5 copy.72
  574.6 11.6 %bitcast_reduce_fusion = f32[128,2048]{0,1:T(8,128)S(1)} fusion(f32[256,8,8,128]{3,2,1,0:T(8,128)S(1)} %copy.72), kind=kLoop, calls=%fused_computation.46 | loop fusion | flops 1835008 | bytes 9437184 | tf_op jit(solution)/shard_map/reduce_sum | solution.py:88
  (202 shorter events, 151.3 us)
Async XLA Ops:
  7.2 163.5 %reduce-scatter.2.cloned.1.call-start = ((), (), s32[]{:S(2)}) async-start(), calls=%async_computation.2 | async-start | bytes 17825792 | tf_op jit(solution)/shard_map/reduce_scatter | solution.py:80
  20.9 149.8 %copy-start = (s32[1,4]{1,0:T(1,128)S(1)}, s32[1,4]{1,0:T(1,128)}, u32[]{:S(2)}) copy-start(s32[1,4]{1,0:T(1,128)} %param.23) | copy-start | bytes 52
  20.9 151.2 %copy-start.8 = (f32[512,16]{0,1:T(8,128)S(1)}, f32[512,16]{0,1:T(8,128)}, u32[]{:S(2)}) copy-start(f32[512,16]{0,1:T(8,128)} %param.22) | copy-start | bytes 98308
  20.9 222.9 %all-gather.4.cloned.1.call-start = ((), (), s32[]{:S(2)}) async-start(), calls=%async_computation.1 | async-start | bytes 8912896 | tf_op jit(solution)/shard_map/all_gather | solution.py:70
  21.6 547.4 %all-gather.6.cloned.1.call-start = ((), (), s32[]{:S(2)}) async-start(), calls=%async_computation.3 | async-start | bytes 9437184 | tf_op jit(solution)/shard_map/all_gather | solution.py:88
  172.1 2.4 copy-start.5
  174.4 2.0 copy-start.6
  180.4 2.5 copy-start.3
  180.4 3.2 copy-start.4
  183.6 60.3 %copy-start.10 = (bf16[512,2048]{1,0:T(8,128)(2,1)S(1)}, bf16[512,2048]{1,0:T(8,128)(2,1)}, u32[]{:S(2)}) copy-start(bf16[512,2048]{1,0:T(8,128)(2,1)} %param.21) | copy-start | bytes 6291460
  252.8 1.6 copy-start.7
  266.5 2.5 copy-start.9
  557.9 2.9 copy-start.2
  562.5 2.9 copy-start.1
Sparse Core Ops, SparseCore 0:
  21.0 149.5 reduce-scatter.1
  173.3 70.4 all-gather.3
  245.5 95.6 all-gather.5

commit v2 on v0

--- a/solution.py
+++ b/solution.py
@@ -67,7 +67,9 @@
     grad_input = jnp.where(token_valid[:, None], out_grad, jnp.zeros_like(out_grad))
     attn_grad = lax.dot_general(
         grad_input,
-        lax.all_gather(out_weight, "fsdp", axis=0, tiled=True),
+        jnp.concatenate(
+            lax.all_to_all(jnp.stack([out_weight] * lax.axis_size("fsdp")), "fsdp", 0, 0), axis=0
+        ),
         (((1,), (1,)), ((), ())),
         preferred_element_type=jnp.float32,
     ).astype(jnp.bfloat16)

time: 487 us -> 588 us (1.21)
  waiting for transfers between devices: 107 us -> 198 us
  starting transfers between devices: 0.3 us -> 8.41 us
    all_to_all x0 -> x1, waiting for transfers between devices: none -> 126 us  [per_device(): lax.all_to_all(jnp.stack([out_weight] * lax.axis_size('fsdp')), 'fsdp', 0...]
    all_gather x1 -> x0, waiting for transfers between devices: 48 us -> none  [per_device(): lax.all_gather(out_weight, 'fsdp', axis=0, tiled=True)]
    psum x1, waiting for transfers between devices: 58.2 us -> 71.8 us  [per_device(): weight_grad = lax.psum(grad_share, 'dp')]
    all_to_all x0 -> x1, starting transfers between devices: none -> 8.15 us  [per_device(): lax.all_to_all(jnp.stack([out_weight] * lax.axis_size('fsdp')), 'fsdp', 0...]
    unnamed x31 -> x33, local copies, waits for them, and re-layouts: 23.6 us -> 22.6 us
  transfers between devices with their start and end apart: 3 -> 3, of which waited for: 2 -> 2; matrix products, arithmetic and copies ran while one was open for 62% -> 49% of each run, Pallas kernels for 0% -> 0%
where the time goes in v2:
time: 588 us; the launch traced here: 584 us
  waiting for transfers between devices  198 us (34%)
  matrix products  193 us (33%)
  local copies, waits for them, and re-layouts  94.9 us (16%)
  loops' own time  51.5 us (9%)
  other arithmetic  23.1 us (4%)
  between operations  14.2 us (2%)
  starting transfers between devices  8.41 us (1%)
    all_to_all x1, waiting for transfers between devices, per_device(): lax.all_to_all(jnp.stack([out_weight] * lax.axis_size('fsdp')), 'fsdp', 0...  126 us
    psum x1, waiting for transfers between devices, per_device(): weight_grad = lax.psum(grad_share, 'dp')  71.8 us
    dot_general x16, matrix products, pair_grads(): jnp.einsum('hqk,hqd->hkd', score_grad, query_heads, preferred_element_typ...  52.5 us
    dot_general x16, matrix products, pair_grads(): jnp.einsum('hqk,hqd->hkd', probs.astype(jnp.bfloat16), grad_heads, prefer...  52.3 us
    another operation x1, loops' own time, per_device(): totals = lax.fori_loop(0, pair_total, run_pair, totals)  51.5 us
    dot_general x16, matrix products, pair_grads(): jnp.einsum('hqk,hkd->hqd', score_grad, key_heads, preferred_element_type=...  50.4 us
    unnamed x33, local copies, waits for them, and re-layouts  22.6 us
    dynamic_slice x16, local copies, waits for them, and re-layouts, take_blocks(): value_blocks[key_block]  22.2 us
  transfers between devices with their start and end apart: 3, of which 2 were waited for; matrix products, arithmetic and copies ran while one was open for 49% of the time, Pallas kernels for 0%

profile of v2, /device:TPU:0, one launch (start us, length us, event | category | flops | bytes accessed | tf_op | source)
XLA Modules:
  0.0 583.7 jit_solution(17467304648238700157)
XLA Ops:
  8.2 12.6 %convolution_bitcast_fusion.1 = f32[2048,2048]{0,1:T(8,128)} fusion(bf16[512,2048]{1,0:T(8,128)(2,1)} %param.20, bf16[512,2048]{1,0:T(8,128)(2,1)} %param.21, pred[512]{0:T(512)(128)(4,1)S(1)} %fusion.27), kind=kOutput, calls=%fused_computation.45 | convolution fusion | flops 4296015872 | bytes 20972032 | tf_op jit(solution)/shard_map/dot_general | solution.py:83
  21.9 4.3 stack.2
  26.2 8.2 %all-to-all-start = ((bf16[16,128,2048]{2,1,0:T(8,128)(2,1)}), bf16[16,128,2048]{2,1,0:T(8,128)(2,1)}, u32[]{:S(2)}, u32[]{:S(2)}) async-start(bf16[16,128,2048]{2,1,0:T(8,128)(2,1)} %stack.2), calls=%async_computation | async-start | bytes 16777216 | tf_op jit(solution)/shard_map/all_to_all | solution.py:71
  50.5 126.5 %all-to-all-done = bf16[16,128,2048]{2,1,0:T(8,128)(2,1)} async-done(((bf16[16,128,2048]{2,1,0:T(8,128)(2,1)}), bf16[16,128,2048]{2,1,0:T(8,128)(2,1)}, u32[]{:S(2)}, u32[]{:S(2)}) %all-to-all-start) | async-done | bytes 8388640 | tf_op jit(solution)/shard_map/all_to_all | solution.py:71
  177.0 8.9 %convolution_convert_fusion = bf16[512,2048]{1,0:T(8,128)(2,1)S(1)} fusion(bf16[2048,2048]{1,0:T(8,128)(2,1)} %bitcast.21, bf16[512,2048]{1,0:T(8,128)(2,1)} %param.21, pred[512]{0:T(512)(128)(4,1)S(1)} %fusion.27), kind=kOutput, calls=%fused_computation.47 | convolution fusion | flops 4297064448 | bytes 12583424 | tf_op jit(solution)/shard_map/dot_general | solution.py:68
  189.5 3.4 reduce_sum.39
  201.5 285.8 %while.19 = (s32[]{:T(128)}, f32[4,16,128,128]{3,2,1,0:T(8,128)}, f32[4,16,128,128]{3,2,1,0:T(8,128)}, f32[4,16,128,128]{3,2,1,0:T(8,128)}, s32[]{:T(128)}, /*in...) while((s32[]{:T(128)}, f32[4,16,128,128]{3,2,1,0:T(8,128)}, ...), condition=%wide.region_8.9_spmd, body=%wide.region_5.8_spmd.sunk | while | flops 339476544 | bytes 17879460 | solution.py:128
  209.8 3.3 fusion.48
  213.1 3.1 fusion.47
  216.3 3.3 fusion.49
  227.7 3.6 fusion.48
  231.3 3.1 fusion.47
  234.4 3.2 fusion.49
  245.8 3.3 fusion.48
  249.1 3.1 fusion.47
  252.2 3.3 fusion.49
  263.6 3.2 fusion.48
  266.8 3.1 fusion.47
  270.0 3.2 fusion.49
  281.3 3.2 fusion.48
  284.6 3.2 fusion.47
  287.7 3.3 fusion.49
  299.2 3.3 fusion.48
  302.5 3.2 fusion.47
  305.7 3.2 fusion.49
  317.0 3.3 fusion.48
  320.3 3.2 fusion.47
  323.5 3.2 fusion.49
  334.8 3.2 fusion.48
  338.1 3.2 fusion.47
  341.2 3.2 fusion.49
  352.6 3.2 fusion.48
  359.0 3.3 fusion.49
  370.4 3.3 fusion.48
  376.8 3.2 fusion.49
  388.2 3.3 fusion.48
  394.6 3.2 fusion.49
  406.0 3.2 fusion.48
  412.3 3.2 fusion.49
  423.7 3.2 fusion.48
  430.1 3.3 fusion.49
  441.5 3.3 fusion.48
  447.9 3.2 fusion.49
  459.3 3.3 fusion.48
  465.7 3.2 fusion.49
  477.0 3.2 fusion.48
  483.4 3.2 fusion.49
  502.5 71.8 %all-reduce.2.cloned.1.call-done = f32[128,2048]{0,1:T(8,128)} async-done(((f32[128,2048]{0,1:T(8,128)}), f32[128,2048]{0,1:T(8,128)}) %all-reduce.2.cloned.1.call-update) | async-done | bytes 1048592 | tf_op jit(solution)/shard_map/psum | solution.py:90
  (202 shorter events, 152.2 us)
Async XLA Ops:
  7.2 480.1 %reduce-scatter.2.cloned.1.call-start = ((), (), s32[]{:S(2)}) async-start(), calls=%async_computation.2 | async-start | bytes 17825792 | tf_op jit(solution)/shard_map/reduce_scatter | solution.py:82
  20.9 1.0 copy-start.9
  26.2 8.4 %copy-start = (s32[1,4]{1,0:T(1,128)S(1)}, s32[1,4]{1,0:T(1,128)}, u32[]{:S(2)}) copy-start(s32[1,4]{1,0:T(1,128)} %param.23) | copy-start | bytes 52
  26.2 9.8 %copy-start.5 = (bf16[512,2048]{1,0:T(8,128)(2,1)S(1)}, bf16[512,2048]{1,0:T(8,128)(2,1)}, u32[]{:S(2)}) copy-start(bf16[512,2048]{1,0:T(8,128)(2,1)} %param.19) | copy-start | bytes 6291460
  26.2 150.7 %all-to-all-start = ((bf16[16,128,2048]{2,1,0:T(8,128)(2,1)}), bf16[16,128,2048]{2,1,0:T(8,128)(2,1)}, u32[]{:S(2)}, u32[]{:S(2)}) async-start(bf16[16,128,2048]{2,1,0:T(8,128)(2,1)} %stack.2), calls=%async_computation | async-start | bytes 16777216 | tf_op jit(solution)/shard_map/all_to_all | solution.py:71
  34.4 540.0 %all-reduce.2.cloned.1.call-start = ((), (), s32[]{:S(2)}) async-start(), calls=%async_computation.3 | async-start | bytes 2097152 | tf_op jit(solution)/shard_map/psum | solution.py:90
  36.0 2.4 copy-start.6
  38.4 2.6 copy-start.7
  41.0 0.8 copy-start.10
  43.7 2.8 copy-start.3
  43.7 3.8 copy-start.4
  177.0 8.9 %copy-start.8 = (bf16[512,2048]{1,0:T(8,128)(2,1)S(1)}, bf16[512,2048]{1,0:T(8,128)(2,1)}, u32[]{:S(2)}) copy-start(bf16[512,2048]{1,0:T(8,128)(2,1)} %param.20) | copy-start | bytes 6291460
  199.0 2.5 copy-start.11
  491.3 2.9 copy-start.2
  496.0 2.9 copy-start.1
Sparse Core Ops, SparseCore 0:
  21.0 234.8 reduce-scatter.1
  487.5 86.8 all-reduce.1
